TPU v7x, 32 devices: a whole 2x2x4 slice. The times are simulated.
32 devices in a mesh: expert: 4 (over y, x), req: 8 (over z, core).
Axes of the slice: x: 2, y: 2, z: 4, core: 2. Of those that a mesh axis runs over, the one named last changes fastest.
Arguments:
- queries: bfloat16 [8192, 1024], P(('expert', 'req')), may hold values from -82 to 82
- self_kv: bfloat16 [8192, 2048], P(('expert', 'req')), may hold values from -4 to 4
- kv_pages: bfloat16 [32, 128, 2048], P(('expert', 'req')), may hold values from -4 to 4
- page_table: int32 [4, 8], P('expert'), may hold values from 0 to 7, as said below
- lengths: int32 [8192], P(('expert', 'req')), may hold values from 1 to 1024
- routes: int32 [8192, 2], P(('expert', 'req')), may hold values from 0 to 3, all different within a row
- residual: bfloat16 [8192, 1024], P(('expert', 'req')), may hold values from -20 to 20
- w_attn_out: bfloat16 [1024, 1024], replicated, may hold values from -0.1875 to 0.1875
- gain_attn: bfloat16 [1024], replicated, may hold values from 0.25 to 1.75
- w_router: bfloat16 [1024, 4], replicated, may hold values from -0.1875 to 0.1875
- w_in: bfloat16 [4, 1024, 2816], P('expert'), may hold values from -0.1875 to 0.1875
- w_out: bfloat16 [4, 1408, 1024], P('expert'), may hold values from -0.15625 to 0.15625
- gain_out: bfloat16 [1024], replicated, may hold values from 0.25 to 1.75
Outputs:
- layer_out: bfloat16 [8192, 1024], P(('expert', 'req'))
Inputs may be any that keep to these rules, and one draw needn't show every extreme that they name: Each row of page_table is a permutation of 0 to 7.
All inputs are finite; a program needn't handle non-finite values.
Results may differ from a plain program's by a relative error of at most 0.01.
Values may be sent and summed in bfloat16 or wider, within the bound.
A program may use at most 128 MiB of HBM per device.

v0:
```python
import math
import jax
import jax.numpy as jnp
from jax import lax
from jax.sharding import PartitionSpec as P

HEADS = 16
HEAD_DIM = 64
TOP = 2
PAGE = 128
HD = 1024
norm_eps = 1e-06


def block_size(total_count, largest):
    chosen = min(total_count, largest)
    while total_count % chosen:
        chosen -= 1
    return chosen


def key_positions(table_row, key_count, page_len):
    logical = jnp.arange(table_row.shape[0], dtype=jnp.int32)
    inverse = jnp.sum(
        jnp.where(table_row[:, None] == logical[None, :], logical[:, None], 0), axis=0
    )
    flat_index = jnp.arange(key_count, dtype=jnp.int32)
    page_index = flat_index // page_len
    logical_page = jnp.sum(
        jnp.where(page_index[:, None] == logical[None, :], inverse[None, :], 0), axis=1
    )
    return logical_page * page_len + flat_index % page_len


def rms_scale(values, gain_row):
    mean_square = jnp.mean(values * values, axis=-1, keepdims=True)
    return values * lax.rsqrt(mean_square + norm_eps) * gain_row.astype(jnp.float32)


def route_block(route_rows, cap_size, expert_count):
    onehot = (
        route_rows[:, :, None] == jnp.arange(expert_count, dtype=jnp.int32)[None, None, :]
    ).astype(jnp.int32)
    ordered = onehot.transpose(1, 0, 2).reshape(-1, expert_count)
    earlier = jnp.cumsum(ordered, axis=0) - ordered
    position = jnp.sum(earlier * ordered, axis=1).reshape(route_rows.shape[1], route_rows.shape[0])
    kept_mask = position < cap_size
    slot_ids = jnp.where(kept_mask, route_rows.T * cap_size + position, -1)
    return (onehot, kept_mask, slot_ids)


def on_device(
    queries,
    self_kv,
    kv_pages,
    page_table,
    lengths,
    routes,
    residual,
    w_attn_out,
    gain_attn,
    w_router,
    w_in,
    w_out,
    gain_out,
):
    row_count = queries.shape[0]
    scale_qk = 1.0 / math.sqrt(HEAD_DIM)
    table_row = page_table[0]
    page_rows = kv_pages.reshape(-1, kv_pages.shape[-1])
    query_h = queries.reshape(row_count, HEADS, HEAD_DIM)
    own_key = self_kv[:, :HD].reshape(row_count, HEADS, HEAD_DIM)
    own_value = self_kv[:, HD:].reshape(row_count, HEADS, HEAD_DIM)
    own_score = (
        jnp.einsum("rhd,rhd->hr", query_h, own_key, preferred_element_type=jnp.float32) * scale_qk
    )
    start_value = jnp.swapaxes(own_value, 0, 1).astype(jnp.float32)
    initial = (own_score, jnp.ones_like(own_score), start_value)
    page_piece = lax.all_gather(page_rows, "req", axis=0, tiled=True)
    piece_len = page_piece.shape[0]
    step_len = block_size(piece_len, 512)
    positions = key_positions(table_row, piece_len, PAGE)
    blocks = page_piece.reshape(piece_len // step_len, step_len, page_piece.shape[1])
    block_pos = positions.reshape(piece_len // step_len, step_len)

    def add_block(running, block_items):
        highest, weight_sum, weighted = running
        block_rows, block_place = block_items
        key_rows = block_rows[:, :HD].reshape(step_len, HEADS, HEAD_DIM)
        value_rows = block_rows[:, HD:].reshape(step_len, HEADS, HEAD_DIM)
        scores = (
            jnp.einsum("rhd,khd->hrk", query_h, key_rows, preferred_element_type=jnp.float32)
            * scale_qk
        )
        visible = block_place[None, :] < lengths[:, None]
        masked = jnp.where(visible[None], scores, -jnp.inf)
        new_high = jnp.maximum(highest, jnp.max(masked, axis=2))
        factor = jnp.exp(highest - new_high)
        weights = jnp.exp(masked - new_high[:, :, None])
        weight_sum = weight_sum * factor + jnp.sum(weights, axis=2)
        weighted = weighted * factor[:, :, None] + jnp.einsum(
            "hrk,khd->hrd",
            weights.astype(jnp.bfloat16),
            value_rows,
            preferred_element_type=jnp.float32,
        )
        return ((new_high, weight_sum, weighted), None)

    result, unused = lax.scan(add_block, initial, (blocks, block_pos))
    highest, weight_sum, weighted = result
    attended = (
        (weighted / weight_sum[:, :, None])
        .transpose(1, 0, 2)
        .reshape(row_count, HD)
        .astype(jnp.bfloat16)
    )
    residual_sum = residual.astype(jnp.float32) + jnp.dot(
        attended, w_attn_out, preferred_element_type=jnp.float32
    )
    normed = rms_scale(residual_sum, gain_attn).astype(jnp.bfloat16)
    logits = jnp.dot(normed, w_router, preferred_element_type=jnp.float32)
    experts_all = w_router.shape[1]
    cap_size = (5 * row_count * TOP + 4 * experts_all - 1) // (4 * experts_all)
    onehot, kept_mask, slot_ids = route_block(routes, cap_size, experts_all)
    picked = jnp.sum(jnp.where(onehot > 0, logits[:, None, :], 0.0), axis=2)
    gate_values = jax.nn.sigmoid(picked - picked[:, ::-1])
    slot_range = jnp.arange(experts_all * cap_size, dtype=jnp.int32)
    assign = jnp.sum(
        (slot_ids[:, None, :] == slot_range[None, :, None]).astype(jnp.bfloat16), axis=0
    )
    model_width = normed.shape[1]
    buffer = (
        jnp.dot(assign, normed, preferred_element_type=jnp.float32)
        .astype(jnp.bfloat16)
        .reshape(experts_all, cap_size, model_width)
    )
    arrived = lax.all_to_all(buffer, "expert", split_axis=0, concat_axis=0, tiled=True)
    slot_count = arrived.shape[1]
    local_experts = w_in.shape[0]
    hidden_width = w_out.shape[1]
    grouped = arrived.reshape(-1, local_experts, slot_count, model_width)
    inner_act = jnp.einsum("slnd,ldf->slnf", grouped, w_in, preferred_element_type=jnp.float32)
    hidden = (
        jax.nn.gelu(inner_act[..., :hidden_width], approximate=True) * inner_act[..., hidden_width:]
    ).astype(jnp.bfloat16)
    outcome = jnp.einsum(
        "slnf,lfd->slnd", hidden, w_out, preferred_element_type=jnp.float32
    ).astype(jnp.bfloat16)
    expert_done = outcome.reshape(-1, slot_count, model_width)
    collected = lax.all_to_all(expert_done, "expert", split_axis=0, concat_axis=0, tiled=True)
    flat_rows = collected.reshape(-1, model_width)
    picked_rows = flat_rows[jnp.maximum(slot_ids, 0)]
    gate_kept = jnp.where(kept_mask, gate_values.T, 0.0)
    mixture = jnp.sum(picked_rows.astype(jnp.float32) * gate_kept[:, :, None], axis=0)
    return rms_scale(residual_sum + mixture, gain_out).astype(jnp.bfloat16)


def solution(mesh):
    in_specs = (
        P(("expert", "req"), None),
        P(("expert", "req"), None),
        P(("expert", "req"), None, None),
        P("expert", None),
        P(("expert", "req")),
        P(("expert", "req"), None),
        P(("expert", "req"), None),
        P(),
        P(),
        P(),
        P("expert", None, None),
        P("expert", None, None),
        P(),
    )
    out_specs = P(("expert", "req"), None)
    return jax.shard_map(
        on_device, mesh=mesh, in_specs=in_specs, out_specs=out_specs, check_vma=False
    )
```

profile of v0, /device:TPU:0, one launch (start us, length us, event | category | flops | bytes accessed | tf_op | source)
XLA Modules:
  0.0 183.3 jit_solution(17256257046171117510)
XLA Ops:
  7.3 2.5 %slice_convert_fusion = (f32[256,1024]{1,0:T(8,128)}, bf16[256,1024]{1,0:T(8,128)(2,1)S(1)}) fusion(bf16[256,2048]{1,0:T(8,128)(2,1)} %param.16), kind=kLoop, calls=%fused_computation.51 | loop fusion | flops 262144 | bytes 2621440 | tf_op jit(solution)/shard_map/convert_element_type | solution.py:77
  12.0 2.6 %copy.29 = f32[256,1024]{0,1:T(8,128)} copy(f32[256,1024]{1,0:T(8,128)} %get-tuple-element.119) | data formatting | bytes 2097152 | tf_op jit(solution)/shard_map/convert_element_type | solution.py:77
  21.2 37.7 %all-gather.3.cloned.1.call-done = bf16[1,1024,2048]{2,1,0:T(8,128)(2,1)} async-done(((bf16[1,128,2048]{2,1,0:T(8,128)(2,1)}), bf16[1,1024,2048]{2,1,0:T(8,128)(2,1)}) %all-gather.3.cloned.1.call-update) | async-done | bytes 4194320 | tf_op jit(solution)/shard_map/all_gather | solution.py:79
  58.9 54.3 %while.15 = (s32[]{:T(128)}, f32[16,256]{1,0:T(8,128)}, f32[16,256]{1,0:T(8,128)}, f32[16,256,64]{1,2,0:T(8,128)}, s32[2,512]{1,0:T(2,128)}, /*index=5*/s32[256]...) while((s32[]{:T(128)}, f32[16,256]{1,0:T(8,128)}, ...), condition=%wide.region_5.6_spmd.clone, body=%wide.region_2.5_spmd.clone.sunk | while | flops 560607232 | bytes 76881064 | solution.py:109
  60.4 3.1 %constant_dynamic-slice_fusion.5 = bf16[1,512,2048]{2,1,0:T(8,128)(2,1)} fusion(bf16[2,512,2048]{2,1,0:T(8,128)(2,1)} %get-tuple-element.210, s32[]{:T(128)} %get-tuple-element.194), kind=kLoop, calls=%fused_computation.13.clone.1 | loop fusion | bytes 4194308 | tf_op jit(solution)/shard_map/while/body/jit(dynamic_index_in_dim)/dynamic_slice | solution.py:109
  63.5 3.9 %copy.48 = bf16[1,512,2048]{1,2,0:T(8,128)(2,1)} copy(bf16[1,512,2048]{2,1,0:T(8,128)(2,1)} %constant_dynamic-slice_fusion.5) | data formatting | bytes 4194304 | tf_op jit(solution)/shard_map/while/body/jit(dynamic_index_in_dim)/dynamic_slice | solution.py:109
  67.4 2.6 %fusion.78 = (bf16[512,1024]{0,1:T(8,128)(2,1)}, bf16[512,1024]{0,1:T(8,128)(2,1)S(1)}) fusion(bf16[512,2048]{0,1:T(8,128)(2,1)} %bitcast.117), kind=kLoop, calls=%fused_computation.94.clone.1 | loop fusion | bytes 4194304 | tf_op jit(solution)/shard_map/while/body/eval_jaxpr/slice | solution.py:90
  71.6 3.2 %copy-done.1 = f32[16,512,256]{2,1,0:T(8,128)} copy-done((f32[16,512,256]{2,1,0:T(8,128)}, f32[16,512,256]{2,1,0:T(8,128)S(1)}, u32[]{:S(2)}) %copy-start.1) | copy-done | bytes 8388632 | tf_op jit(solution)/shard_map/while
  74.8 2.3 %fusion.80 = f32[16,256]{1,0:T(8,128)} fusion(f32[16,512,256]{2,1,0:T(8,128)S(1)} %get-tuple-element.180, f32[16,256]{1,0:T(8,128)S(1)} %max.10, pred[256,512]{0,1:T(8,128)(4,1)S(1)} %broadcast_compare_fusion.3), kind=kLoop, calls=%fused_computation.4.clone.1 | loop fusion | flops 8384512 | bytes 8552448 | tf_op jit(solution)/shard_map/while/body/eval_jaxpr/reduce_sum | solution.py:100
  78.4 7.0 %fusion.82 = f32[16,256,64]{1,2,0:T(8,128)} fusion(bf16[512,16,64]{0,2,1:T(8,128)(2,1)} %bitcast.120, f32[16,512,256]{2,1,0:T(8,128)} %copy-done.1, f32[16,256]{1,0:T(8,128)S(1)} %max.10, pred[256,512]{0,1:T(8,128)(4,1)S(1)} %broadcast_compare_fusion.3, f32[16,256,64]{1,2,0:T(8,128)} %get-tuple-element.197, f32[16,256]{1,0:T(8,128)S(1)} %get-tuple-element.183), kind=kOutput, calls=%fused_computation.8.clone.1 | convolution fusion | flops 277348352 | bytes 11698176 | tf_op jit(solution)/shard_map/while/body/eval_jaxpr/hrk,khd->hrd/dot_general | solution.py:101
  87.5 3.1 %constant_dynamic-slice_fusion.5 = bf16[1,512,2048]{2,1,0:T(8,128)(2,1)} fusion(bf16[2,512,2048]{2,1,0:T(8,128)(2,1)} %get-tuple-element.210, s32[]{:T(128)} %get-tuple-element.194), kind=kLoop, calls=%fused_computation.13.clone.1 | loop fusion | bytes 4194308 | tf_op jit(solution)/shard_map/while/body/jit(dynamic_index_in_dim)/dynamic_slice | solution.py:109
  90.7 3.9 %copy.48 = bf16[1,512,2048]{1,2,0:T(8,128)(2,1)} copy(bf16[1,512,2048]{2,1,0:T(8,128)(2,1)} %constant_dynamic-slice_fusion.5) | data formatting | bytes 4194304 | tf_op jit(solution)/shard_map/while/body/jit(dynamic_index_in_dim)/dynamic_slice | solution.py:109
  94.6 2.6 %fusion.78 = (bf16[512,1024]{0,1:T(8,128)(2,1)}, bf16[512,1024]{0,1:T(8,128)(2,1)S(1)}) fusion(bf16[512,2048]{0,1:T(8,128)(2,1)} %bitcast.117), kind=kLoop, calls=%fused_computation.94.clone.1 | loop fusion | bytes 4194304 | tf_op jit(solution)/shard_map/while/body/eval_jaxpr/slice | solution.py:90
  98.8 3.2 %copy-done.1 = f32[16,512,256]{2,1,0:T(8,128)} copy-done((f32[16,512,256]{2,1,0:T(8,128)}, f32[16,512,256]{2,1,0:T(8,128)S(1)}, u32[]{:S(2)}) %copy-start.1) | copy-done | bytes 8388632 | tf_op jit(solution)/shard_map/while
  102.0 2.3 %fusion.80 = f32[16,256]{1,0:T(8,128)} fusion(f32[16,512,256]{2,1,0:T(8,128)S(1)} %get-tuple-element.180, f32[16,256]{1,0:T(8,128)S(1)} %max.10, pred[256,512]{0,1:T(8,128)(4,1)S(1)} %broadcast_compare_fusion.3), kind=kLoop, calls=%fused_computation.4.clone.1 | loop fusion | flops 8384512 | bytes 8552448 | tf_op jit(solution)/shard_map/while/body/eval_jaxpr/reduce_sum | solution.py:100
  105.6 7.0 %fusion.82 = f32[16,256,64]{1,2,0:T(8,128)} fusion(bf16[512,16,64]{0,2,1:T(8,128)(2,1)} %bitcast.120, f32[16,512,256]{2,1,0:T(8,128)} %copy-done.1, f32[16,256]{1,0:T(8,128)S(1)} %max.10, pred[256,512]{0,1:T(8,128)(4,1)S(1)} %broadcast_compare_fusion.3, f32[16,256,64]{1,2,0:T(8,128)} %get-tuple-element.197, f32[16,256]{1,0:T(8,128)S(1)} %get-tuple-element.183), kind=kOutput, calls=%fused_computation.8.clone.1 | convolution fusion | flops 277348352 | bytes 11698176 | tf_op jit(solution)/shard_map/while/body/eval_jaxpr/hrk,khd->hrd/dot_general | solution.py:101
  114.7 2.7 %multiply_reduce_fusion.1 = (f32[256]{0:T(256)S(1)}, f32[256,1024]{1,0:T(8,128)S(1)}) fusion(bf16[256,1024]{0,1:T(8,128)(2,1)S(1)} %bitcast.125, bf16[1024,1024]{1,0:T(8,128)(2,1)} %param.22, bf16[256,1024]{1,0:T(8,128)(2,1)} %param.21), kind=kOutput, calls=%fused_computation.48 | convolution fusion | flops 537919232 | bytes 4195328 | tf_op jit(solution)/shard_map/dot_general | solution.py:117
  119.0 20.8 %all_to_all.10 = bf16[4,160,1024]{2,1,0:T(8,128)(2,1)S(1)} all-to-all(bf16[4,160,1024]{2,1,0:T(8,128)(2,1)S(1)} %bitcast.122), channel_id=1, replica_groups=mesh['expert'=4,'req'=8] {'expert'}, dimensions={0} | all-to-all | bytes 2621440 | tf_op jit(solution)/shard_map/all_to_all | solution.py:137
  139.8 3.9 %fusion.14 = f32[4,1,160,2816]{3,2,0,1:T(8,128)S(1)} fusion(bf16[4,160,1024]{2,1,0:T(8,128)(2,1)S(1)} %all_to_all.10, bf16[1,1024,2816]{2,1,0:T(8,128)(2,1)S(1)} %bitcast.133), kind=kOutput, calls=%fused_computation.20 | convolution fusion | flops 3690987520 | bytes 14286848 | tf_op jit(solution)/shard_map/slnd,ldf->slnf/dot_general | solution.py:142
  143.7 3.6 %fusion.34 = bf16[4,160,1024]{2,1,0:T(8,128)(2,1)} fusion(bf16[1,1408,1024]{2,1,0:T(8,128)(2,1)S(1)} %copy-done, f32[4,1,160,2816]{3,2,0,1:T(8,128)S(1)} %fusion.14), kind=kOutput, calls=%fused_computation.39 | convolution fusion | flops 1855160320 | bytes 11403264 | tf_op jit(solution)/shard_map/slnf,lfd->slnd/dot_general | solution.py:146
  147.4 4.4 %all-to-all-start.1 = ((bf16[4,160,1024]{2,1,0:T(8,128)(2,1)}), bf16[4,160,1024]{2,1,0:T(8,128)(2,1)}, u32[]{:S(2)}, u32[]{:S(2)}) async-start(bf16[4,160,1024]{2,1,0:T(8,128)(2,1)} %fusion.34), calls=%async_computation.1 | async-start | bytes 2621440 | tf_op jit(solution)/shard_map/all_to_all | solution.py:150
  153.6 13.9 %all-to-all-done.1 = bf16[4,160,1024]{2,1,0:T(8,128)(2,1)} async-done(((bf16[4,160,1024]{2,1,0:T(8,128)(2,1)}), bf16[4,160,1024]{2,1,0:T(8,128)(2,1)}, u32[]{:S(2)}, u32[]{:S(2)}) %all-to-all-start.1) | async-done | bytes 1310752 | tf_op jit(solution)/shard_map/all_to_all | solution.py:150
  167.5 5.0 %gather_fusion = bf16[512,1024]{1,0:T(8,128)(2,1)} fusion(bf16[640,1024]{1,0:T(8,128)(2,1)} %bitcast.26, s32[1024]{0:T(1024)S(1)} %pad_clamp_fusion), kind=kCustom, calls=%fused_computation | custom fusion | bytes 2099200 | tf_op jit(solution)/shard_map/gather | solution.py:152
  172.5 1.6 fusion.28
  (87 shorter events, 26.6 us)
Async XLA Ops:
  6.5 137.2 %copy-start = (bf16[1,1408,1024]{2,1,0:T(8,128)(2,1)S(1)}, bf16[1,1408,1024]{2,1,0:T(8,128)(2,1)}, u32[]{:S(2)}) copy-start(bf16[1,1408,1024]{2,1,0:T(8,128)(2,1)} %param.26) | copy-start | bytes 8650756
  6.5 8.1 %copy-start.14 = (s32[1,8]{1,0:T(1,128)S(1)}, s32[1,8]{1,0:T(1,128)}, u32[]{:S(2)}) copy-start(s32[1,8]{1,0:T(1,128)} %param.18) | copy-start | bytes 100
  6.5 8.3 %copy-start.12 = (bf16[1024]{0:T(1024)(128)(2,1)S(1)}, bf16[1024]{0:T(1024)(128)(2,1)}, u32[]{:S(2)}) copy-start(bf16[1024]{0:T(1024)(128)(2,1)} %param.23) | copy-start | bytes 6148
  6.5 8.8 %copy-start.6 = (s32[256,2]{0,1:T(2,128)S(1)}, s32[256,2]{0,1:T(2,128)}, u32[]{:S(2)}) copy-start(s32[256,2]{0,1:T(2,128)} %param.20) | copy-start | bytes 6148
  6.5 52.3 %all-gather.3.cloned.1.call-start = ((), (), s32[]{:S(2)}) async-start(), calls=%async_computation.2 | async-start | bytes 4718592 | tf_op jit(solution)/shard_map/all_gather | solution.py:79
  17.1 41.7 %copy-start.8 = (s32[2,256]{1,0:T(2,128)}, s32[2,256]{1,0:T(2,128)S(1)}, u32[]{:S(2)}) copy-start(s32[2,256]{1,0:T(2,128)S(1)} %reshape.142) | copy-start | bytes 6148
  70.1 1.5 copy-start.3
  71.6 3.2 %copy-start.1 = (f32[16,512,256]{2,1,0:T(8,128)}, f32[16,512,256]{2,1,0:T(8,128)S(1)}, u32[]{:S(2)}) copy-start(f32[16,512,256]{2,1,0:T(8,128)S(1)} %get-tuple-element.180) | copy-start | bytes 25165828 | tf_op jit(solution)/shard_map/while
  97.2 1.5 copy-start.3
  98.7 3.2 %copy-start.1 = (f32[16,512,256]{2,1,0:T(8,128)}, f32[16,512,256]{2,1,0:T(8,128)S(1)}, u32[]{:S(2)}) copy-start(f32[16,512,256]{2,1,0:T(8,128)S(1)} %get-tuple-element.180) | copy-start | bytes 25165828 | tf_op jit(solution)/shard_map/while
  113.2 5.2 %copy-start.4 = (bf16[640,256]{1,0:T(8,128)(2,1)S(1)}, bf16[640,256]{1,0:T(8,128)(2,1)}, u32[]{:S(2)}) copy-start(bf16[640,256]{1,0:T(8,128)(2,1)} %fusion.41) | copy-start | bytes 983044
  113.2 5.2 %copy-start.5 = (f32[1024]{0:T(1024)S(1)}, f32[1024]{0:T(1024)}, u32[]{:S(2)}) copy-start(f32[1024]{0:T(1024)} %convert_element_type.77) | copy-start | bytes 12292
  113.2 26.6 %slice-start = ((s8[5767168]{0:T(1024)(128)(4,1)}), s8[4194304]{0:T(1024)(128)(4,1)S(1)}, s32[]{:S(2)}) async-start(s8[5767168]{0:T(1024)(128)(4,1)} %bitcast.132), calls=%async_computation.3 | async-start | bytes 8388608
  114.7 25.1 %slice-start.1 = ((s8[5767168]{0:T(1024)(128)(4,1)}), s8[1572864]{0:T(1024)(128)(4,1)S(1)}, s32[]{:S(2)}) async-start(s8[5767168]{0:T(1024)(128)(4,1)} %bitcast.132), calls=%async_computation.4 | async-start | bytes 3145728
  117.4 1.0 copy-start.2
  143.7 8.1 %copy-start.11 = (s32[1,2,2,128]{3,2,1,0:T(2,128)S(1)}, s32[1,2,2,128]{3,2,1,0:T(2,128)}, u32[]{:S(2)}) copy-start(s32[1,2,2,128]{3,2,1,0:T(2,128)} %get-tuple-element.113) | copy-start | bytes 6148
  143.7 8.1 %copy-start.13 = (bf16[1024]{0:T(1024)(128)(2,1)S(1)}, bf16[1024]{0:T(1024)(128)(2,1)}, u32[]{:S(2)}) copy-start(bf16[1024]{0:T(1024)(128)(2,1)} %param.27) | copy-start | bytes 6148
  143.7 8.1 %copy-start.10 = (bf16[1024,4]{0,1:T(4,128)(2,1)S(1)}, bf16[1024,4]{0,1:T(4,128)(2,1)}, u32[]{:S(2)}) copy-start(bf16[1024,4]{0,1:T(4,128)(2,1)} %param.24) | copy-start | bytes 24580
  147.4 6.0 %copy-start.7 = (s32[256,2]{0,1:T(2,128)S(1)}, s32[256,2]{0,1:T(2,128)}, u32[]{:S(2)}) copy-start(s32[256,2]{0,1:T(2,128)} %param.20) | copy-start | bytes 6148
  147.4 6.1 %copy-start.9 = (s32[2,256]{1,0:T(2,128)S(1)}, s32[2,256]{1,0:T(2,128)}, u32[]{:S(2)}) copy-start(s32[2,256]{1,0:T(2,128)} %copy-done.8) | copy-start | bytes 6148
  147.4 20.1 %all-to-all-start.1 = ((bf16[4,160,1024]{2,1,0:T(8,128)(2,1)}), bf16[4,160,1024]{2,1,0:T(8,128)(2,1)}, u32[]{:S(2)}, u32[]{:S(2)}) async-start(bf16[4,160,1024]{2,1,0:T(8,128)(2,1)} %fusion.34), calls=%async_computation.1 | async-start | bytes 2621440 | tf_op jit(solution)/shard_map/all_to_all | solution.py:150
Sparse Core Ops, SparseCore 0:
  9.0 49.8 all-gather.2
where the time goes:
time: 184 us; the launch traced here: 183 us
  waiting for transfers between devices  52.3 us (28%)
  local copies, waits for them, and re-layouts  39.6 us (22%)
  matrix products  29.3 us (16%)
  other arithmetic  23.2 us (13%)
  blocking collectives  20.8 us (11%)
  between operations  13.6 us (7%)
  starting transfers between devices  4.44 us (2%)
    all_gather x1, waiting for transfers between devices, on_device(): page_piece = lax.all_gather(page_rows, 'req', axis=0, tiled=True)  37.7 us
    all_to_all x1, blocking collectives, on_device(): lax.all_to_all(buffer, 'expert', split_axis=0, concat_axis=0, tiled=True)  20.8 us
    dynamic_slice x6, local copies, waits for them, and re-layouts, on_device(): result, unused = lax.scan(add_block, initial, (blocks, block_pos))  15.5 us
    dot_general x2, matrix products, add_block(): jnp.einsum('hrk,khd->hrd', weights.astype(jnp.bfloat16), value_rows, pref...  14 us
    all_to_all x1, waiting for transfers between devices, on_device(): lax.all_to_all(expert_done, 'expert', split_axis=0, concat_axis=0, tiled=...  13.9 us
    while x10, local copies, waits for them, and re-layouts  7.6 us
    slice x2, local copies, waits for them, and re-layouts, add_block(): value_rows = block_rows[:, HD:].reshape(step_len, HEADS, HEAD_DIM)  5.29 us
    gather x1, local copies, waits for them, and re-layouts, on_device(): picked_rows = flat_rows[jnp.maximum(slot_ids, 0)]  4.97 us
  transfers between devices with their start and end apart: 2, of which 2 were waited for; matrix products, arithmetic and copies ran while one was open for 8% of the time, Pallas kernels for 0%

commit v1 on v0

--- a/solution.py
+++ b/solution.py
@@ -10,6 +10,24 @@
 PAGE = 128
 HD = 1024
 norm_eps = 1e-06
+
+
+def gather_around(shard, axis, dim):
+    ways, here, lap = (lax.axis_size(axis), lax.axis_index(axis), shard.shape[dim])
+    shape = [n * ways if d == dim else n for d, n in enumerate(shard.shape)]
+    full = lax.dynamic_update_slice_in_dim(
+        jnp.zeros(shape, shard.dtype), shard, here * lap, axis=dim
+    )
+    going_up = going_down = shard
+    for far in range(1, ways // 2 + 1):
+        going_up = lax.ppermute(going_up, axis, [(d, (d + 1) % ways) for d in range(ways)])
+        full = lax.dynamic_update_slice_in_dim(full, going_up, (here - far) % ways * lap, axis=dim)
+        if 2 * far < ways:
+            going_down = lax.ppermute(going_down, axis, [(d, (d - 1) % ways) for d in range(ways)])
+            full = lax.dynamic_update_slice_in_dim(
+                full, going_down, (here + far) % ways * lap, axis=dim
+            )
+    return full
 
 
 def block_size(total_count, largest):
@@ -76,7 +94,7 @@
     )
     start_value = jnp.swapaxes(own_value, 0, 1).astype(jnp.float32)
     initial = (own_score, jnp.ones_like(own_score), start_value)
-    page_piece = lax.all_gather(page_rows, "req", axis=0, tiled=True)
+    page_piece = gather_around(page_rows, "req", 0)
     piece_len = page_piece.shape[0]
     step_len = block_size(piece_len, 512)
     positions = key_positions(table_row, piece_len, PAGE)

time: 184 us -> 169 us (0.918)
  the two profiles are of different devices: /device:TPU:0 before, /device:TPU:8 now
where the time goes in v1:
time: 169 us; the launch traced here: 168 us
  local copies, waits for them, and re-layouts  53.1 us (31%)
  matrix products  29.3 us (17%)
  waiting for transfers between devices  25.2 us (15%)
  other arithmetic  23 us (14%)
  blocking collectives  22 us (13%)
  starting transfers between devices  15.2 us (9%)
    all_to_all x1, blocking collectives, on_device(): lax.all_to_all(buffer, 'expert', split_axis=0, concat_axis=0, tiled=True)  22 us
    dynamic_slice x6, local copies, waits for them, and re-layouts, on_device(): result, unused = lax.scan(add_block, initial, (blocks, block_pos))  15.5 us
    all_to_all x1, waiting for transfers between devices, on_device(): lax.all_to_all(expert_done, 'expert', split_axis=0, concat_axis=0, tiled=...  15.3 us
    dot_general x2, matrix products, add_block(): jnp.einsum('hrk,khd->hrd', weights.astype(jnp.bfloat16), value_rows, pref...  14 us
    ppermute x4, waiting for transfers between devices, gather_around(): lax.ppermute(going_up, axis, [(d, (d + 1) % ways) for d in range(ways)])  8.47 us
    while x10, local copies, waits for them, and re-layouts  7.59 us
    ppermute x4, starting transfers between devices, gather_around(): lax.ppermute(going_up, axis, [(d, (d + 1) % ways) for d in range(ways)])  7.37 us
    dynamic_update_slice x4, local copies, waits for them, and re-layouts, gather_around(): lax.dynamic_update_slice_in_dim(full, going_up, (here - far) % ways * lap...  5.56 us
  transfers between devices with their start and end apart: 8, of which 5 were waited for; matrix products, arithmetic and copies ran while one was open for 17% of the time, Pallas kernels for 0%

profile of v1, /device:TPU:8, one launch (start us, length us, event | category | flops | bytes accessed | tf_op | source)
XLA Modules:
  0.0 168.2 jit_solution(13422913978136165710)
XLA Ops:
  1.8 2.3 %slice_convert_fusion = (f32[256,1024]{1,0:T(8,128)}, bf16[256,1024]{1,0:T(8,128)(2,1)S(1)}) fusion(bf16[256,2048]{1,0:T(8,128)(2,1)} %param.16), kind=kLoop, calls=%fused_computation.51 | loop fusion | flops 262144 | bytes 2621440 | tf_op jit(solution)/shard_map/convert_element_type | solution.py:95
  12.4 2.5 %broadcast_in_dim.91 = bf16[1024,2048]{1,0:T(8,128)(2,1)} broadcast(bf16[]{:T(256)} %constant.115.clone.1), dimensions={} | broadcast | bytes 4194306 | tf_op jit(solution)/shard_map/broadcast_in_dim | solution.py:19
  18.6 2.6 %copy.29 = f32[256,1024]{0,1:T(8,128)} copy(f32[256,1024]{1,0:T(8,128)} %get-tuple-element.119) | data formatting | bytes 2097152 | tf_op jit(solution)/shard_map/convert_element_type | solution.py:95
  21.8 4.6 %collective-permute-start.4 = (bf16[128,2048]{1,0:T(8,128)(2,1)}, bf16[128,2048]{1,0:T(8,128)(2,1)S(1)}, u32[]{:S(2)}, u32[]{:S(2)}) collective-permute-start(bf16[128,2048]{1,0:T(8,128)(2,1)} %collective-permute-done.2), channel_id=1, source_target_pairs={{0,1},{1,2},{2,3},{3,4},{4,5},{5,6},{6,7},{7,0},{8,9},{9,10},{10,1... | collective-permute-start | bytes 1572872 | tf_op jit(solution)/shard_map/ppermute | solution.py:23
  33.6 2.7 %collective-permute-start.6 = (bf16[128,2048]{1,0:T(8,128)(2,1)S(1)}, bf16[128,2048]{1,0:T(8,128)(2,1)S(1)}, u32[]{:S(2)}, u32[]{:S(2)}) collective-permute-start(bf16[128,2048]{1,0:T(8,128)(2,1)S(1)} %collective-permute-done.4), channel_id=1, source_target_pairs={{0,1},{1,2},{2,3},{3,4},{4,5},{5,6},{6,7},{7,0},{8,9},{9,10},{10,1... | collective-permute-start | bytes 1572872 | tf_op jit(solution)/shard_map/ppermute | solution.py:23
  41.3 6.0 %collective-permute-done.6 = bf16[128,2048]{1,0:T(8,128)(2,1)S(1)} collective-permute-done((bf16[128,2048]{1,0:T(8,128)(2,1)S(1)}, bf16[128,2048]{1,0:T(8,128)(2,1)S(1)}, u32[]{:S(2)}, u32[]{:S(2)}) %collective-permute-start.6) | collective-permute-done | bytes 524320 | tf_op jit(solution)/shard_map/ppermute | solution.py:23
  48.1 54.4 %while.15 = (s32[]{:T(128)}, f32[16,256]{1,0:T(8,128)}, f32[16,256]{1,0:T(8,128)}, f32[16,256,64]{1,2,0:T(8,128)}, s32[2,512]{1,0:T(2,128)}, /*index=5*/s32[256]...) while((s32[]{:T(128)}, f32[16,256]{1,0:T(8,128)}, ...), condition=%wide.region_5.6_spmd.clone, body=%wide.region_2.5_spmd.clone.sunk | while | flops 560607232 | bytes 76881064 | solution.py:127
  49.7 3.1 %constant_dynamic-slice_fusion.5 = bf16[1,512,2048]{2,1,0:T(8,128)(2,1)} fusion(bf16[2,512,2048]{2,1,0:T(8,128)(2,1)} %get-tuple-element.210, s32[]{:T(128)} %get-tuple-element.194), kind=kLoop, calls=%fused_computation.13.clone.1 | loop fusion | bytes 4194308 | tf_op jit(solution)/shard_map/while/body/jit(dynamic_index_in_dim)/dynamic_slice | solution.py:127
  52.8 3.9 %copy.48 = bf16[1,512,2048]{1,2,0:T(8,128)(2,1)} copy(bf16[1,512,2048]{2,1,0:T(8,128)(2,1)} %constant_dynamic-slice_fusion.5) | data formatting | bytes 4194304 | tf_op jit(solution)/shard_map/while/body/jit(dynamic_index_in_dim)/dynamic_slice | solution.py:127
  56.7 2.6 %fusion.78 = (bf16[512,1024]{0,1:T(8,128)(2,1)}, bf16[512,1024]{0,1:T(8,128)(2,1)S(1)}) fusion(bf16[512,2048]{0,1:T(8,128)(2,1)} %bitcast.119), kind=kLoop, calls=%fused_computation.102.clone.1 | loop fusion | bytes 4194304 | tf_op jit(solution)/shard_map/while/body/eval_jaxpr/slice | solution.py:108
  60.9 3.2 %copy-done.1 = f32[16,512,256]{2,1,0:T(8,128)} copy-done((f32[16,512,256]{2,1,0:T(8,128)}, f32[16,512,256]{2,1,0:T(8,128)S(1)}, u32[]{:S(2)}) %copy-start.1) | copy-done | bytes 8388632 | tf_op jit(solution)/shard_map/while
  67.7 7.0 %fusion.82 = f32[16,256,64]{1,2,0:T(8,128)} fusion(bf16[512,16,64]{0,2,1:T(8,128)(2,1)} %bitcast.121, f32[16,512,256]{2,1,0:T(8,128)} %copy-done.1, f32[16,256]{1,0:T(8,128)S(1)} %max.10, pred[256,512]{0,1:T(8,128)(4,1)S(1)} %broadcast_compare_fusion.3, f32[16,256,64]{1,2,0:T(8,128)} %get-tuple-element.197, f32[16,256]{1,0:T(8,128)S(1)} %get-tuple-element.183), kind=kOutput, calls=%fused_computation.8.clone.1 | convolution fusion | flops 277348352 | bytes 11698176 | tf_op jit(solution)/shard_map/while/body/eval_jaxpr/hrk,khd->hrd/dot_general | solution.py:119
  76.8 3.1 %constant_dynamic-slice_fusion.5 = bf16[1,512,2048]{2,1,0:T(8,128)(2,1)} fusion(bf16[2,512,2048]{2,1,0:T(8,128)(2,1)} %get-tuple-element.210, s32[]{:T(128)} %get-tuple-element.194), kind=kLoop, calls=%fused_computation.13.clone.1 | loop fusion | bytes 4194308 | tf_op jit(solution)/shard_map/while/body/jit(dynamic_index_in_dim)/dynamic_slice | solution.py:127
  80.0 3.9 %copy.48 = bf16[1,512,2048]{1,2,0:T(8,128)(2,1)} copy(bf16[1,512,2048]{2,1,0:T(8,128)(2,1)} %constant_dynamic-slice_fusion.5) | data formatting | bytes 4194304 | tf_op jit(solution)/shard_map/while/body/jit(dynamic_index_in_dim)/dynamic_slice | solution.py:127
  83.9 2.6 %fusion.78 = (bf16[512,1024]{0,1:T(8,128)(2,1)}, bf16[512,1024]{0,1:T(8,128)(2,1)S(1)}) fusion(bf16[512,2048]{0,1:T(8,128)(2,1)} %bitcast.119), kind=kLoop, calls=%fused_computation.102.clone.1 | loop fusion | bytes 4194304 | tf_op jit(solution)/shard_map/while/body/eval_jaxpr/slice | solution.py:108
  88.1 3.2 %copy-done.1 = f32[16,512,256]{2,1,0:T(8,128)} copy-done((f32[16,512,256]{2,1,0:T(8,128)}, f32[16,512,256]{2,1,0:T(8,128)S(1)}, u32[]{:S(2)}) %copy-start.1) | copy-done | bytes 8388632 | tf_op jit(solution)/shard_map/while
  94.9 7.0 %fusion.82 = f32[16,256,64]{1,2,0:T(8,128)} fusion(bf16[512,16,64]{0,2,1:T(8,128)(2,1)} %bitcast.121, f32[16,512,256]{2,1,0:T(8,128)} %copy-done.1, f32[16,256]{1,0:T(8,128)S(1)} %max.10, pred[256,512]{0,1:T(8,128)(4,1)S(1)} %broadcast_compare_fusion.3, f32[16,256,64]{1,2,0:T(8,128)} %get-tuple-element.197, f32[16,256]{1,0:T(8,128)S(1)} %get-tuple-element.183), kind=kOutput, calls=%fused_computation.8.clone.1 | convolution fusion | flops 277348352 | bytes 11698176 | tf_op jit(solution)/shard_map/while/body/eval_jaxpr/hrk,khd->hrd/dot_general | solution.py:119
  104.0 2.7 %multiply_reduce_fusion.1 = (f32[256]{0:T(256)S(1)}, f32[256,1024]{1,0:T(8,128)S(1)}) fusion(bf16[256,1024]{0,1:T(8,128)(2,1)S(1)} %bitcast.126, bf16[1024,1024]{1,0:T(8,128)(2,1)} %param.22, bf16[256,1024]{1,0:T(8,128)(2,1)} %param.21), kind=kOutput, calls=%fused_computation.48 | convolution fusion | flops 537919232 | bytes 4195328 | tf_op jit(solution)/shard_map/dot_general | solution.py:135
  108.3 22.0 %all_to_all.10 = bf16[4,160,1024]{2,1,0:T(8,128)(2,1)S(1)} all-to-all(bf16[4,160,1024]{2,1,0:T(8,128)(2,1)S(1)} %bitcast.123), channel_id=1, replica_groups=mesh['expert'=4,'req'=8] {'expert'}, dimensions={0} | all-to-all | bytes 2621440 | tf_op jit(solution)/shard_map/all_to_all | solution.py:155
  130.3 3.9 %fusion.14 = f32[4,1,160,2816]{3,2,0,1:T(8,128)S(1)} fusion(bf16[4,160,1024]{2,1,0:T(8,128)(2,1)S(1)} %all_to_all.10, bf16[1,1024,2816]{2,1,0:T(8,128)(2,1)S(1)} %bitcast.136), kind=kOutput, calls=%fused_computation.20 | convolution fusion | flops 3690987520 | bytes 14286848 | tf_op jit(solution)/shard_map/slnd,ldf->slnf/dot_general | solution.py:160
  134.3 3.6 %fusion.34 = bf16[4,160,1024]{2,1,0:T(8,128)(2,1)} fusion(bf16[1,1408,1024]{2,1,0:T(8,128)(2,1)S(1)} %copy-done, f32[4,1,160,2816]{3,2,0,1:T(8,128)S(1)} %fusion.14), kind=kOutput, calls=%fused_computation.39 | convolution fusion | flops 1855160320 | bytes 11403264 | tf_op jit(solution)/shard_map/slnf,lfd->slnd/dot_general | solution.py:164
  137.9 4.3 %all-to-all-start.1 = ((bf16[4,160,1024]{2,1,0:T(8,128)(2,1)}), bf16[4,160,1024]{2,1,0:T(8,128)(2,1)}, u32[]{:S(2)}, u32[]{:S(2)}) async-start(bf16[4,160,1024]{2,1,0:T(8,128)(2,1)} %fusion.34), calls=%async_computation.1 | async-start | bytes 2621440 | tf_op jit(solution)/shard_map/all_to_all | solution.py:168
  143.9 15.3 %all-to-all-done.1 = bf16[4,160,1024]{2,1,0:T(8,128)(2,1)} async-done(((bf16[4,160,1024]{2,1,0:T(8,128)(2,1)}), bf16[4,160,1024]{2,1,0:T(8,128)(2,1)}, u32[]{:S(2)}, u32[]{:S(2)}) %all-to-all-start.1) | async-done | bytes 1310752 | tf_op jit(solution)/shard_map/all_to_all | solution.py:168
  159.3 5.0 %gather_fusion = bf16[512,1024]{1,0:T(8,128)(2,1)} fusion(bf16[640,1024]{1,0:T(8,128)(2,1)} %bitcast.27, s32[1024]{0:T(1024)S(1)} %pad_clamp_fusion), kind=kCustom, calls=%fused_computation | custom fusion | bytes 2099200 | tf_op jit(solution)/shard_map/gather | solution.py:170
  (109 shorter events, 50.5 us)
Async XLA Ops:
  0.0 134.2 %copy-start = (bf16[1,1408,1024]{2,1,0:T(8,128)(2,1)S(1)}, bf16[1,1408,1024]{2,1,0:T(8,128)(2,1)}, u32[]{:S(2)}) copy-start(bf16[1,1408,1024]{2,1,0:T(8,128)(2,1)} %param.26) | copy-start | bytes 8650756
  0.0 6.4 %copy-start.15 = (s32[1,8]{1,0:T(1,128)S(1)}, s32[1,8]{1,0:T(1,128)}, u32[]{:S(2)}) copy-start(s32[1,8]{1,0:T(1,128)} %param.18) | copy-start | bytes 100
  0.0 7.2 %copy-start.7 = (s32[256,2]{0,1:T(2,128)S(1)}, s32[256,2]{0,1:T(2,128)}, u32[]{:S(2)}) copy-start(s32[256,2]{0,1:T(2,128)} %param.20) | copy-start | bytes 6148
  0.0 12.4 %collective-permute-start = (bf16[128,2048]{1,0:T(8,128)(2,1)}, bf16[128,2048]{1,0:T(8,128)(2,1)}, u32[]{:S(2)}, u32[]{:S(2)}) collective-permute-start(bf16[128,2048]{1,0:T(8,128)(2,1)} %bitcast.127), channel_id=1, source_target_pairs={{0,1},{1,2},{2,3},{3,4},{4,5},{5,6},{6,7},{7,0},{8,9},{9,10},{10,1... | collective-permute-start | bytes 1572872 | tf_op jit(solution)/shard_map/ppermute | solution.py:23
  0.1 15.7 %collective-permute-start.1 = (bf16[128,2048]{1,0:T(8,128)(2,1)}, bf16[128,2048]{1,0:T(8,128)(2,1)}, u32[]{:S(2)}, u32[]{:S(2)}) collective-permute-start(bf16[128,2048]{1,0:T(8,128)(2,1)} %bitcast.128), channel_id=1, source_target_pairs={{0,7},{1,0},{2,1},{3,2},{4,3},{5,4},{6,5},{7,6},{8,15},{9,8},{10,9... | collective-permute-start | bytes 1572872 | tf_op jit(solution)/shard_map/ppermute | solution.py:26
  10.1 11.0 %copy-start.13 = (bf16[1024]{0:T(1024)(128)(2,1)S(1)}, bf16[1024]{0:T(1024)(128)(2,1)}, u32[]{:S(2)}) copy-start(bf16[1024]{0:T(1024)(128)(2,1)} %param.23) | copy-start | bytes 6148
  10.2 18.2 %copy-start.9 = (s32[2,256]{1,0:T(2,128)}, s32[2,256]{1,0:T(2,128)S(1)}, u32[]{:S(2)}) copy-start(s32[2,256]{1,0:T(2,128)S(1)} %reshape.142) | copy-start | bytes 6148
  11.4 3.6 %copy-start.5 = (bf16[1,128,2048]{2,1,0:T(8,128)(2,1)S(1)}, bf16[1,128,2048]{2,1,0:T(8,128)(2,1)}, u32[]{:S(2)}) copy-start(bf16[1,128,2048]{2,1,0:T(8,128)(2,1)} %param.17) | copy-start | bytes 1572868
  12.4 9.3 %collective-permute-start.2 = (bf16[128,2048]{1,0:T(8,128)(2,1)}, bf16[128,2048]{1,0:T(8,128)(2,1)}, u32[]{:S(2)}, u32[]{:S(2)}) collective-permute-start(bf16[128,2048]{1,0:T(8,128)(2,1)} %collective-permute-done), channel_id=1, source_target_pairs={{0,1},{1,2},{2,3},{3,4},{4,5},{5,6},{6,7},{7,0},{8,9},{9,10},{10,1... | collective-permute-start | bytes 1572872 | tf_op jit(solution)/shard_map/ppermute | solution.py:23
  15.8 14.5 %collective-permute-start.3 = (bf16[128,2048]{1,0:T(8,128)(2,1)}, bf16[128,2048]{1,0:T(8,128)(2,1)}, u32[]{:S(2)}, u32[]{:S(2)}) collective-permute-start(bf16[128,2048]{1,0:T(8,128)(2,1)} %collective-permute-done.1), channel_id=1, source_target_pairs={{0,7},{1,0},{2,1},{3,2},{4,3},{5,4},{6,5},{7,6},{8,15},{9,8},{10,9... | collective-permute-start | bytes 1572872 | tf_op jit(solution)/shard_map/ppermute | solution.py:26
  21.8 11.9 %collective-permute-start.4 = (bf16[128,2048]{1,0:T(8,128)(2,1)}, bf16[128,2048]{1,0:T(8,128)(2,1)S(1)}, u32[]{:S(2)}, u32[]{:S(2)}) collective-permute-start(bf16[128,2048]{1,0:T(8,128)(2,1)} %collective-permute-done.2), channel_id=1, source_target_pairs={{0,1},{1,2},{2,3},{3,4},{4,5},{5,6},{6,7},{7,0},{8,9},{9,10},{10,1... | collective-permute-start | bytes 1572872 | tf_op jit(solution)/shard_map/ppermute | solution.py:23
  30.2 10.2 %collective-permute-start.5 = (bf16[128,2048]{1,0:T(8,128)(2,1)}, bf16[128,2048]{1,0:T(8,128)(2,1)S(1)}, u32[]{:S(2)}, u32[]{:S(2)}) collective-permute-start(bf16[128,2048]{1,0:T(8,128)(2,1)} %collective-permute-done.3), channel_id=1, source_target_pairs={{0,7},{1,0},{2,1},{3,2},{4,3},{5,4},{6,5},{7,6},{8,15},{9,8},{10,9... | collective-permute-start | bytes 1572872 | tf_op jit(solution)/shard_map/ppermute | solution.py:26
  33.6 13.7 %collective-permute-start.6 = (bf16[128,2048]{1,0:T(8,128)(2,1)S(1)}, bf16[128,2048]{1,0:T(8,128)(2,1)S(1)}, u32[]{:S(2)}, u32[]{:S(2)}) collective-permute-start(bf16[128,2048]{1,0:T(8,128)(2,1)S(1)} %collective-permute-done.4), channel_id=1, source_target_pairs={{0,1},{1,2},{2,3},{3,4},{4,5},{5,6},{6,7},{7,0},{8,9},{9,10},{10,1... | collective-permute-start | bytes 1572872 | tf_op jit(solution)/shard_map/ppermute | solution.py:23
  88.0 3.2 %copy-start.1 = (f32[16,512,256]{2,1,0:T(8,128)}, f32[16,512,256]{2,1,0:T(8,128)S(1)}, u32[]{:S(2)}) copy-start(f32[16,512,256]{2,1,0:T(8,128)S(1)} %get-tuple-element.180) | copy-start | bytes 25165828 | tf_op jit(solution)/shard_map/while
  102.5 5.2 %copy-start.4 = (bf16[640,256]{1,0:T(8,128)(2,1)S(1)}, bf16[640,256]{1,0:T(8,128)(2,1)}, u32[]{:S(2)}) copy-start(bf16[640,256]{1,0:T(8,128)(2,1)} %fusion.41) | copy-start | bytes 983044
  102.5 5.2 %copy-start.6 = (f32[1024]{0:T(1024)S(1)}, f32[1024]{0:T(1024)}, u32[]{:S(2)}) copy-start(f32[1024]{0:T(1024)} %convert_element_type.77) | copy-start | bytes 12292
  102.5 27.8 %slice-start = ((s8[5767168]{0:T(1024)(128)(4,1)}), s8[4194304]{0:T(1024)(128)(4,1)S(1)}, s32[]{:S(2)}) async-start(s8[5767168]{0:T(1024)(128)(4,1)} %bitcast.135), calls=%async_computation.2 | async-start | bytes 8388608
  104.0 26.3 %slice-start.1 = ((s8[5767168]{0:T(1024)(128)(4,1)}), s8[1572864]{0:T(1024)(128)(4,1)S(1)}, s32[]{:S(2)}) async-start(s8[5767168]{0:T(1024)(128)(4,1)} %bitcast.135), calls=%async_computation.3 | async-start | bytes 3145728
  134.2 8.0 %copy-start.12 = (s32[1,2,2,128]{3,2,1,0:T(2,128)S(1)}, s32[1,2,2,128]{3,2,1,0:T(2,128)}, u32[]{:S(2)}) copy-start(s32[1,2,2,128]{3,2,1,0:T(2,128)} %get-tuple-element.113) | copy-start | bytes 6148
  134.2 8.0 %copy-start.14 = (bf16[1024]{0:T(1024)(128)(2,1)S(1)}, bf16[1024]{0:T(1024)(128)(2,1)}, u32[]{:S(2)}) copy-start(bf16[1024]{0:T(1024)(128)(2,1)} %param.27) | copy-start | bytes 6148
  134.2 8.0 %copy-start.11 = (bf16[1024,4]{0,1:T(4,128)(2,1)S(1)}, bf16[1024,4]{0,1:T(4,128)(2,1)}, u32[]{:S(2)}) copy-start(bf16[1024,4]{0,1:T(4,128)(2,1)} %param.24) | copy-start | bytes 24580
  134.2 9.6 %copy-start.8 = (s32[256,2]{0,1:T(2,128)S(1)}, s32[256,2]{0,1:T(2,128)}, u32[]{:S(2)}) copy-start(s32[256,2]{0,1:T(2,128)} %param.20) | copy-start | bytes 6148
  134.2 9.7 %copy-start.10 = (s32[2,256]{1,0:T(2,128)S(1)}, s32[2,256]{1,0:T(2,128)}, u32[]{:S(2)}) copy-start(s32[2,256]{1,0:T(2,128)} %copy-done.9) | copy-start | bytes 6148
  137.9 21.4 %all-to-all-start.1 = ((bf16[4,160,1024]{2,1,0:T(8,128)(2,1)}), bf16[4,160,1024]{2,1,0:T(8,128)(2,1)}, u32[]{:S(2)}, u32[]{:S(2)}) async-start(bf16[4,160,1024]{2,1,0:T(8,128)(2,1)} %fusion.34), calls=%async_computation.1 | async-start | bytes 2621440 | tf_op jit(solution)/shard_map/all_to_all | solution.py:168
  (4 other events, 7.2 us)
